TPU v7x, 256 devices: a whole 4x4x8 slice. The times are simulated.
256 devices in a mesh: slide: 64 (over z, y, core), grp: 4 (over x).
Axes of the slice: x: 4, y: 4, z: 8, core: 2. Of those that a mesh axis runs over, the one named last changes fastest.
Arguments:
- features: bfloat16 [1024, 131072], P('grp', 'slide'), may hold values from -6 to 6
- tissue: int32 [256, 32], P('slide'), may hold values 0 or 1
- group_owner: int32 [8192, 1], P('slide'), may hold values from 0 to 63; in each aligned block of 128 rows (0 to 127, 128 to 255, ...) at most 4 rows name the same one
- reduce_weight: bfloat16 [256, 1024], P(None, 'grp'), may hold values from -0.1875 to 0.1875
- spatial_weight: bfloat16 [9, 256, 256], P(None, 'grp'), may hold values from -0.125 to 0.125
- expand_weight: bfloat16 [1024, 256], P('grp'), may hold values from -0.375 to 0.375
- reduce_scale: float32 [256], P('grp'), may hold values from 0.25 to 1.75
- reduce_shift: float32 [256], P('grp'), may hold values from -2.5 to 2.5
- spatial_scale: float32 [256], P('grp'), may hold values from 0.25 to 1.75
- spatial_shift: float32 [256], P('grp'), may hold values from -2.5 to 2.5
- expand_scale: float32 [1024], P('grp'), may hold values from 0.25 to 1.75
- expand_shift: float32 [1024], P('grp'), may hold values from -2.5 to 2.5
- upstream: bfloat16 [1024, 131072], P('grp', 'slide'), may hold values from -6 to 6
Outputs:
- merged: bfloat16 [4096, 65536], P('grp', 'slide')
- feature_grad: bfloat16 [1024, 131072], P('grp', 'slide')
- reduce_grad: float32 [256, 1024], P(None, 'grp')
- spatial_grad: float32 [9, 256, 256], P(None, 'grp')
- expand_grad: float32 [1024, 256], P('grp')
Inputs may be any that keep to these rules, and one draw needn't show every extreme that they name: `group_owner`: among the 128 tiles of one device, no device is named more than 4 times.
All inputs are finite; a program needn't handle non-finite values. No bound on the sum of `tissue` on one device may be relied on, other than what follows from the above.
Results may differ from a plain program's by a relative error of at most 0.03.
Values may be sent and summed in bfloat16 or wider, within the bound.
No kernel may reach another device: no remote copies, remote signals or barrier semaphores. Data moves between devices by JAX's collectives and lax.ppermute only.
A program may use at most 128 MiB of HBM per device.

v0:
```python
import math

import jax
import jax.numpy as jnp
from jax import lax
from jax.sharding import PartitionSpec as P

GRID_C = 8


tap_offsets = ((-1, -1), (-1, 0), (-1, 1), (0, -1), (0, 0), (0, 1), (1, -1), (1, 0), (1, 1))
neighbour_steps = ((-1, -1), (-1, 0), (-1, 1), (0, -1), (0, 1), (1, -1), (1, 0), (1, 1))


def passed_along(block, axis, distance):
    devices = range(lax.axis_size(axis))
    route = [(i - distance, i) for i in devices if i - distance in devices]
    return lax.ppermute(block, axis, route)


def gelu_fn(values):
    return jax.nn.gelu(values, approximate=True)


def gelu_back(values, cotangent):
    return jax.vjp(gelu_fn, values)[1](cotangent)[0]


def window_taps(padded, direction, height, breadth):
    pieces = []
    for offset_pair in tap_offsets:
        row_start = 1 + direction * offset_pair[0]
        col_start = 1 + direction * offset_pair[1]
        pieces.append(
            padded[:, row_start : row_start + height, col_start : col_start + breadth].reshape(
                padded.shape[0], height * breadth
            )
        )
    return jnp.stack(pieces, 0)


def neighbour_present(devices):
    grid_rows = devices // GRID_C
    own_index = lax.axis_index("slide")
    region_row = own_index // GRID_C
    region_col = own_index % GRID_C
    present = []
    for offset_pair in neighbour_steps:
        row_there = region_row + offset_pair[0]
        col_there = region_col + offset_pair[1]
        present.append(
            (row_there >= 0) & (row_there < grid_rows) & (col_there >= 0) & (col_there < GRID_C)
        )
    return present


def pick_edge(region_block, toward_row, toward_col):
    if toward_row < 0:
        row_part = region_block[:, :1]
    elif toward_row > 0:
        row_part = region_block[:, -1:]
    else:
        row_part = region_block
    if toward_col < 0:
        edge_part = row_part[:, :, :1]
    elif toward_col > 0:
        edge_part = row_part[:, :, -1:]
    else:
        edge_part = row_part
    return edge_part.reshape(region_block.shape[0], -1)


def surround(region_block, present, mover):
    strips = []
    for position, offset_pair in enumerate(neighbour_steps):
        outgoing = pick_edge(region_block, -offset_pair[0], -offset_pair[1])
        arrived = mover(outgoing, -(offset_pair[0] * GRID_C + offset_pair[1]))
        strips.append(arrived * present[position].astype(arrived.dtype))
    (
        upper_left,
        upper_edge,
        upper_right,
        left_edge,
        right_edge,
        lower_left,
        lower_edge,
        lower_right,
    ) = strips
    top_row = jnp.concatenate([upper_left, upper_edge, upper_right], 1)
    bottom = jnp.concatenate([lower_left, lower_edge, lower_right], 1)
    middle = jnp.concatenate([left_edge[:, :, None], region_block, right_edge[:, :, None]], 2)
    return jnp.concatenate([top_row[:, None], middle, bottom[:, None]], 1)


def shards(
    features,
    tissue,
    group_owner,
    reduce_weight,
    spatial_weight,
    expand_weight,
    reduce_scale,
    reduce_shift,
    spatial_scale,
    spatial_shift,
    expand_scale,
    expand_shift,
    upstream,
):
    slide_count = lax.axis_size("slide")
    tile_rows, tile_cols = tissue.shape
    height = 4 * tile_rows
    breadth = 4 * tile_cols
    cell_count = height * breadth
    mid_share = reduce_weight.shape[0] // lax.axis_size("grp")
    cell_mask = (
        jnp.repeat(jnp.repeat(tissue, 4, 0), 4, 1).reshape(1, cell_count).astype(jnp.float32)
    )
    present = neighbour_present(slide_count)
    reduced = lax.psum_scatter(
        jnp.dot(reduce_weight, features, preferred_element_type=jnp.float32).astype(jnp.bfloat16),
        "grp",
        scatter_dimension=0,
        tiled=True,
    ).astype(jnp.float32)
    pre_first = reduce_scale[:, None] * reduced + reduce_shift[:, None]
    first_act = (cell_mask * gelu_fn(pre_first)).astype(jnp.bfloat16)
    first_grid = first_act.reshape(mid_share, height, breadth)
    first_all = lax.all_gather(first_grid, "grp", axis=0, tiled=True)
    padded = surround(first_all, present, lambda strip, step: passed_along(strip, "slide", step))
    columns = window_taps(padded, 1, height, breadth)
    pre_second = (
        spatial_scale[:, None]
        * jnp.einsum("toi,tin->on", spatial_weight, columns, preferred_element_type=jnp.float32)
        + spatial_shift[:, None]
    )
    second_act = (cell_mask * gelu_fn(pre_second)).astype(jnp.bfloat16)
    second_all = lax.all_gather(second_act, "grp", axis=0, tiled=True)
    expanded = jnp.dot(expand_weight, second_all, preferred_element_type=jnp.float32)
    pre_out = (
        features.astype(jnp.float32) + expand_scale[:, None] * expanded + expand_shift[:, None]
    )
    output = (cell_mask * gelu_fn(pre_out)).astype(jnp.bfloat16)
    quarter = output.shape[0]
    group_blocks = (
        output.reshape(quarter, tile_rows, 2, 2, tile_cols, 2, 2)
        .transpose(0, 3, 6, 1, 4, 2, 5)
        .reshape(quarter * 4, -1, 4)
    )
    group_count = group_blocks.shape[1]
    per_peer = max(2, 2 * group_count // slide_count)
    destination = group_owner[:, 0]
    owner_hits = (destination[:, None] == jnp.arange(slide_count, dtype=jnp.int32)[None, :]).astype(
        jnp.int32
    )
    arrival_rank = jnp.sum(jnp.cumsum(owner_hits, 0) * owner_hits, 1) - 1
    slot_of = destination * per_peer + arrival_rank
    slot_match = slot_of[:, None] == jnp.arange(slide_count * per_peer, dtype=jnp.int32)[None, :]
    source_group = jnp.sum(
        jnp.where(slot_match, jnp.arange(group_count, dtype=jnp.int32)[:, None], 0), 0
    )
    filled = jnp.any(slot_match, 0)
    source_group = jnp.where(filled, source_group, group_count)
    padded_groups = jnp.concatenate([group_blocks, jnp.zeros((quarter * 4, 1, 4), jnp.bfloat16)], 1)
    outgoing_groups = jnp.take(padded_groups, source_group, axis=1).reshape(
        quarter * 4, slide_count * per_peer * 4
    )
    merged = lax.all_to_all(outgoing_groups, "slide", split_axis=1, concat_axis=1, tiled=True)
    err_three = gelu_back(pre_out, cell_mask * upstream.astype(jnp.float32))
    back_three = (expand_scale[:, None] * err_three).astype(jnp.bfloat16)
    expand_part = jnp.einsum(
        "cn,mn->cm", back_three, second_all, preferred_element_type=jnp.float32
    )
    back_second = lax.psum_scatter(
        jnp.einsum(
            "cm,cn->mn", expand_weight, back_three, preferred_element_type=jnp.float32
        ).astype(jnp.bfloat16),
        "grp",
        scatter_dimension=0,
        tiled=True,
    ).astype(jnp.float32)
    err_two = gelu_back(pre_second, cell_mask * back_second)
    back_two = (spatial_scale[:, None] * err_two).astype(jnp.bfloat16)
    spatial_part = jnp.einsum("on,tin->toi", back_two, columns, preferred_element_type=jnp.float32)
    back_grid = back_two.reshape(mid_share, height, breadth)
    back_padded = surround(
        back_grid, present, lambda strip, step: passed_along(strip, "slide", step)
    )
    back_columns = window_taps(back_padded, -1, height, breadth)
    back_first = lax.psum_scatter(
        jnp.einsum(
            "toi,ton->in", spatial_weight, back_columns, preferred_element_type=jnp.float32
        ).astype(jnp.bfloat16),
        "grp",
        scatter_dimension=0,
        tiled=True,
    ).astype(jnp.float32)
    err_one = gelu_back(pre_first, cell_mask * back_first)
    back_one = (reduce_scale[:, None] * err_one).astype(jnp.bfloat16)
    back_one_all = lax.all_gather(back_one, "grp", axis=0, tiled=True)
    reduce_part = jnp.einsum(
        "mn,cn->mc", back_one_all, features, preferred_element_type=jnp.float32
    )
    feature_grad = (
        err_three
        + jnp.einsum("mc,mn->cn", reduce_weight, back_one_all, preferred_element_type=jnp.float32)
    ).astype(jnp.bfloat16)
    reduce_part, spatial_part, expand_part = lax.psum(
        (reduce_part, spatial_part, expand_part), "slide"
    )
    grad_scale = 1.0 / math.sqrt(slide_count * cell_count)
    return (
        merged,
        feature_grad,
        reduce_part * grad_scale,
        spatial_part * grad_scale,
        expand_part * grad_scale,
    )


def solution(mesh):
    return jax.shard_map(
        shards,
        mesh=mesh,
        in_specs=(
            P("grp", "slide"),
            P("slide", None),
            P("slide", None),
            P(None, "grp"),
            P(None, "grp", None),
            P("grp", None),
            P("grp"),
            P("grp"),
            P("grp"),
            P("grp"),
            P("grp"),
            P("grp"),
            P("grp", "slide"),
        ),
        out_specs=(
            P("grp", "slide"),
            P("grp", "slide"),
            P(None, "grp"),
            P(None, "grp", None),
            P("grp", None),
        ),
        check_vma=False,
    )
```

profile of v0, /device:TPU:2, one launch (start us, length us, event | category | flops | bytes accessed | tf_op | source)
XLA Modules:
  0.0 531.3 jit_solution(4127466502366551931)
XLA Ops:
  7.3 2.7 convolution_convert_fusion.1
  10.4 27.9 %reduce-scatter.4.cloned.1.call-done = bf16[64,2048]{1,0:T(8,128)(2,1)} async-done(((bf16[256,2048]{1,0:T(8,128)(2,1)}), bf16[64,2048]{1,0:T(8,128)(2,1)}) %reduce-scatter.4.cloned.1.call-update) | async-done | bytes 262160 | tf_op jit(solution)/shard_map/reduce_scatter | solution.py:120
  40.5 27.6 %all-gather.4.cloned.1.call-done = bf16[256,16,128]{2,1,0:T(8,128)(2,1)} async-done(((bf16[64,16,128]{2,1,0:T(8,128)(2,1)}), bf16[256,16,128]{2,1,0:T(8,128)(2,1)}) %all-gather.4.cloned.1.call-update) | async-done | bytes 1048592 | tf_op jit(solution)/shard_map/all_gather | solution.py:129
  75.5 9.2 %collective-permute-start.1 = (bf16[256,128]{0,1:T(8,128)(2,1)}, bf16[256,128]{0,1:T(8,128)(2,1)}, u32[]{:S(2)}, u32[]{:S(2)}) collective-permute-start(bf16[256,128]{0,1:T(8,128)(2,1)} %bitcast.5), channel_id=1, source_target_pairs={{0,32},{4,36},{8,40},{12,44},{16,48},{20,52},{24,56},{28,60},{32,6... | collective-permute-start | bytes 196616 | tf_op jit(solution)/shard_map/ppermute | solution.py:18
  92.2 4.5 collective-permute-start
  100.3 4.4 collective-permute-done.5
  107.6 2.5 pad_maximum_fusion
  110.1 2.5 pad_maximum_fusion.2
  112.5 3.6 copy.222
  121.4 3.8 pad_maximum_fusion.1
  136.0 2.5 constant_dynamic-update-slice_fusion.7
  145.8 6.4 %multiply_convert_fusion.2 = (bf16[64,2048]{1,0:T(8,128)(2,1)}, f32[64,2048]{1,0:T(8,128)S(1)}) fusion(f32[2048]{0:T(1024)S(1)} %convert_element_type.105, f32[64]{0:T(128)S(1)} %copy-done.28, bf16[9,64,256]{2,1,0:T(8,128)(2,1)S(1)} %copy-done, bf16[9,256,2048]{2,1,0:T(8,128)(2,1)} %constant_dynamic-update-slice_fusion, f32[64]{0:T(128)S(1)} %copy-done.24), kind=kOutput, calls=%fused_computation.69 | convolution fusion | flops 605552640 | bytes 10527232 | tf_op jit(solution)/shard_map/toi,tin->on/dot_general | solution.py:134
  152.3 11.9 %reduce-scatter.6.cloned.1.call-start = ((), (), s32[]{:S(2)}) async-start(), calls=%async_computation.7 | async-start | bytes 1310720 | tf_op jit(solution)/shard_map/reduce_scatter | solution.py:174
  166.8 14.2 %all-gather.6.cloned.1.call-done = bf16[256,2048]{1,0:T(8,128)(2,1)} async-done(((bf16[64,2048]{1,0:T(8,128)(2,1)}), bf16[256,2048]{1,0:T(8,128)(2,1)}) %all-gather.6.cloned.1.call-update) | async-done | bytes 1048592 | tf_op jit(solution)/shard_map/all_gather | solution.py:138
  181.0 3.8 fusion.16
  188.5 24.7 %reduce-scatter.6.cloned.1.call-done = bf16[64,2048]{1,0:T(8,128)(2,1)} async-done(((bf16[256,2048]{1,0:T(8,128)(2,1)}), bf16[64,2048]{1,0:T(8,128)(2,1)}) %reduce-scatter.6.cloned.1.call-update) | async-done | bytes 262160 | tf_op jit(solution)/shard_map/reduce_scatter | solution.py:174
  221.1 7.7 %collective-permute-start.15 = (bf16[64,1]{1,0:T(8,128)(2,1)S(1)}, bf16[64,1]{1,0:T(8,128)(2,1)S(1)}, u32[]{:S(2)}, u32[]{:S(2)}) collective-permute-start(bf16[64,1]{1,0:T(8,128)(2,1)S(1)} %copy.255), channel_id=1, source_target_pairs={{0,28},{4,32},{8,36},{12,40},{16,44},{20,48},{24,52},{28,56},{32,6... | collective-permute-start | bytes 392 | tf_op jit(solution)/shard_map/ppermute | solution.py:18
  231.6 6.2 %collective-permute-start.13 = (bf16[64,1]{0,1:T(2,128)(2,1)S(1)}, bf16[64,1]{0,1:T(2,128)(2,1)S(1)}, u32[]{:S(2)}, u32[]{:S(2)}) collective-permute-start(bf16[64,1]{0,1:T(2,128)(2,1)S(1)} %bitcast.153), channel_id=1, source_target_pairs={{0,36},{4,40},{8,44},{12,48},{16,52},{20,56},{24,60},{28,64},{32,6... | collective-permute-start | bytes 392 | tf_op jit(solution)/shard_map/ppermute | solution.py:18
  237.8 5.3 collective-permute-start.14
  257.7 3.7 fusion.7
  262.1 5.8 %copy.236 = bf16[256,4,2,2,32,2,2]{4,1,6,3,0,5,2:T(4,128)(2,1)} copy(bf16[256,4,2,2,32,2,2]{0,6,5,4,3,2,1:T(2,128)(2,1)S(1)} %reshape.149) | data formatting | bytes 2097152 | tf_op jit(solution)/shard_map/reshape | solution.py:146
  267.9 5.2 reshape.150
  274.4 2.4 gather_fusion
  278.9 3.2 broadcast_select_fusion
  282.0 13.8 %all-to-all-start = ((bf16[1024,64,16]{0,2,1:T(8,128)(2,1)}), bf16[1024,64,16]{0,2,1:T(8,128)(2,1)}, u32[]{:S(2)}, u32[]{:S(2)}) async-start(bf16[1024,64,16]{0,2,1:T(8,128)(2,1)} %broadcast_select_fusion), calls=%async_computation.1 | async-start | bytes 4194304 | tf_op jit(solution)/shard_map/all_to_all | solution.py:168
  299.7 7.6 %convolution_bitcast_fusion.3 = f32[9,64,256]{2,1,0:T(8,128)} fusion(bf16[9,256,2048]{2,1,0:T(8,128)(2,1)} %constant_dynamic-update-slice_fusion, bf16[64,2048]{1,0:T(8,128)(2,1)S(1)} %copy-done.16), kind=kOutput, calls=%fused_computation.34 | convolution fusion | flops 603979776 | bytes 10289152 | tf_op jit(solution)/shard_map/on,tin->toi/dot_general | solution.py:184
  307.3 18.4 %all-gather.8.cloned.1.call-done = bf16[256,2048]{1,0:T(8,128)(2,1)} async-done(((bf16[64,2048]{1,0:T(8,128)(2,1)}), bf16[256,2048]{1,0:T(8,128)(2,1)}) %all-gather.8.cloned.1.call-update) | async-done | bytes 1048592 | tf_op jit(solution)/shard_map/all_gather | solution.py:200
  325.7 2.4 fusion.52
  328.1 19.0 %all-to-all-done = bf16[1024,64,16]{0,2,1:T(8,128)(2,1)} async-done(((bf16[1024,64,16]{0,2,1:T(8,128)(2,1)}), bf16[1024,64,16]{0,2,1:T(8,128)(2,1)}, u32[]{:S(2)}, u32[]{:S(2)}) %all-to-all-start) | async-done | bytes 2097184 | tf_op jit(solution)/shard_map/all_to_all | solution.py:168
  347.1 4.0 copy.259
  351.1 2.4 fusion.5
  355.8 163.2 %all-reduce.4.cloned.1.call-done = (f32[256,256]{1,0:T(8,128)}, f32[9,64,256]{2,1,0:T(8,128)}, f32[256,256]{1,0:T(8,128)}) async-done(((f32[256,256]{1,0:T(8,128)}, f32[9,64,256]{2,1,0:T(8,128)}, f32[256,256]{1,0:T(8,128)}), (f32[256,256]{1,0:T(8,128)}, f32[9,64,256]{2,1,0:T(8,128)}, f32[256,256]{1,0:T(8,128)})) %all-reduce.4.cloned.1.call-update) | async-done | bytes 1114128 | tf_op jit(solution)/shard_map/psum | solution.py:208
  (226 shorter events, 93.6 us)
Async XLA Ops:
  7.2 138.7 %copy-start = (bf16[9,64,256]{2,1,0:T(8,128)(2,1)S(1)}, bf16[9,64,256]{2,1,0:T(8,128)(2,1)}, u32[]{:S(2)}) copy-start(bf16[9,64,256]{2,1,0:T(8,128)(2,1)} %param.17) | copy-start | bytes 884740
  7.2 31.1 %copy-start.27 = (f32[64]{0:T(128)S(1)}, f32[64]{0:T(128)}, u32[]{:S(2)}) copy-start(f32[64]{0:T(128)} %param.19) | copy-start | bytes 772
  7.2 31.1 %copy-start.26 = (f32[64]{0:T(128)S(1)}, f32[64]{0:T(128)}, u32[]{:S(2)}) copy-start(f32[64]{0:T(128)} %param.20) | copy-start | bytes 772
  7.2 31.1 %reduce-scatter.4.cloned.1.call-start = ((), (), s32[]{:S(2)}) async-start(), calls=%async_computation.4 | async-start | bytes 1310720 | tf_op jit(solution)/shard_map/reduce_scatter | solution.py:120
  10.0 58.1 %all-gather.4.cloned.1.call-start = ((), (), s32[]{:S(2)}) async-start(), calls=%async_computation.5 | async-start | bytes 1310720 | tf_op jit(solution)/shard_map/all_gather | solution.py:129
  40.4 140.6 %all-gather.6.cloned.1.call-start = ((), (), s32[]{:S(2)}) async-start(), calls=%async_computation.6 | async-start | bytes 1310720 | tf_op jit(solution)/shard_map/all_gather | solution.py:138
  71.1 34.5 %collective-permute-start.3 = (bf16[256,16]{0,1:T(8,128)(2,1)S(1)}, bf16[256,16]{0,1:T(8,128)(2,1)S(1)}, u32[]{:S(2)}, u32[]{:S(2)}) collective-permute-start(bf16[256,16]{0,1:T(8,128)(2,1)S(1)} %bitcast.143), channel_id=1, source_target_pairs={{0,4},{4,8},{8,12},{12,16},{16,20},{20,24},{24,28},{28,32},{32,36}... | collective-permute-start | bytes 24584 | tf_op jit(solution)/shard_map/ppermute | solution.py:18
  73.3 33.3 %collective-permute-start.4 = (bf16[256,16]{0,1:T(8,128)(2,1)S(1)}, bf16[256,16]{0,1:T(8,128)(2,1)S(1)}, u32[]{:S(2)}, u32[]{:S(2)}) collective-permute-start(bf16[256,16]{0,1:T(8,128)(2,1)S(1)} %bitcast.142), channel_id=1, source_target_pairs={{4,0},{8,4},{12,8},{16,12},{20,16},{24,20},{28,24},{32,28},{36,32}... | collective-permute-start | bytes 24584 | tf_op jit(solution)/shard_map/ppermute | solution.py:18
  75.5 45.1 %collective-permute-start.1 = (bf16[256,128]{0,1:T(8,128)(2,1)}, bf16[256,128]{0,1:T(8,128)(2,1)}, u32[]{:S(2)}, u32[]{:S(2)}) collective-permute-start(bf16[256,128]{0,1:T(8,128)(2,1)} %bitcast.5), channel_id=1, source_target_pairs={{0,32},{4,36},{8,40},{12,44},{16,48},{20,52},{24,56},{28,60},{32,6... | collective-permute-start | bytes 196616 | tf_op jit(solution)/shard_map/ppermute | solution.py:18
  86.6 5.6 %collective-permute-start.7 = (bf16[256,1]{1,0:T(8,128)(2,1)S(1)}, bf16[256,1]{1,0:T(8,128)(2,1)S(1)}, u32[]{:S(2)}, u32[]{:S(2)}) collective-permute-start(bf16[256,1]{1,0:T(8,128)(2,1)S(1)} %bitcast.137), channel_id=1, source_target_pairs={{36,0},{40,4},{44,8},{48,12},{52,16},{56,20},{60,24},{64,28},{68,3... | collective-permute-start | bytes 1544 | tf_op jit(solution)/shard_map/ppermute | solution.py:18
  87.9 9.5 %collective-permute-start.2 = (bf16[256,1]{0,1:T(2,128)(2,1)S(1)}, bf16[256,1]{0,1:T(2,128)(2,1)S(1)}, u32[]{:S(2)}, u32[]{:S(2)}) collective-permute-start(bf16[256,1]{0,1:T(2,128)(2,1)S(1)} %reshape.143), channel_id=1, source_target_pairs={{0,28},{4,32},{8,36},{12,40},{16,44},{20,48},{24,52},{28,56},{32,6... | collective-permute-start | bytes 1544 | tf_op jit(solution)/shard_map/ppermute | solution.py:18
  92.2 6.5 %collective-permute-start = (bf16[256,1]{0,1:T(2,128)(2,1)S(1)}, bf16[256,1]{0,1:T(2,128)(2,1)S(1)}, u32[]{:S(2)}, u32[]{:S(2)}) collective-permute-start(bf16[256,1]{0,1:T(2,128)(2,1)S(1)} %reshape.141), channel_id=1, source_target_pairs={{0,36},{4,40},{8,44},{12,48},{16,52},{20,56},{24,60},{28,64},{32,6... | collective-permute-start | bytes 1544 | tf_op jit(solution)/shard_map/ppermute | solution.py:18
  97.3 20.6 %collective-permute-start.6 = (bf16[256,128]{1,0:T(8,128)(2,1)}, bf16[256,128]{1,0:T(8,128)(2,1)}, u32[]{:S(2)}, u32[]{:S(2)}) collective-permute-start(bf16[256,128]{1,0:T(8,128)(2,1)} %bitcast.118), channel_id=1, source_target_pairs={{32,0},{36,4},{40,8},{44,12},{48,16},{52,20},{56,24},{60,28},{64,3... | collective-permute-start | bytes 196616 | tf_op jit(solution)/shard_map/ppermute | solution.py:18
  98.7 6.1 %collective-permute-start.5 = (bf16[256,1]{0,1:T(2,128)(2,1)S(1)}, bf16[256,1]{0,1:T(2,128)(2,1)S(1)}, u32[]{:S(2)}, u32[]{:S(2)}) collective-permute-start(bf16[256,1]{0,1:T(2,128)(2,1)S(1)} %reshape.146), channel_id=1, source_target_pairs={{28,0},{32,4},{36,8},{40,12},{44,16},{48,20},{52,24},{56,28},{60,3... | collective-permute-start | bytes 1544 | tf_op jit(solution)/shard_map/ppermute | solution.py:18
  152.2 28.8 %copy-start.21 = (bf16[256,256]{1,0:T(8,128)(2,1)S(1)}, bf16[256,256]{1,0:T(8,128)(2,1)}, u32[]{:S(2)}) copy-start(bf16[256,256]{1,0:T(8,128)(2,1)} %param.18) | copy-start | bytes 393220
  152.2 28.7 %copy-start.22 = (f32[256]{0:T(256)S(1)}, f32[256]{0:T(256)}, u32[]{:S(2)}) copy-start(f32[256]{0:T(256)} %param.23) | copy-start | bytes 3076
  152.3 28.7 %copy-start.29 = (f32[256]{0:T(256)S(1)}, f32[256]{0:T(256)}, u32[]{:S(2)}) copy-start(f32[256]{0:T(256)} %param.24) | copy-start | bytes 3076
  152.3 60.9 %reduce-scatter.6.cloned.1.call-start = ((), (), s32[]{:S(2)}) async-start(), calls=%async_computation.7 | async-start | bytes 1310720 | tf_op jit(solution)/shard_map/reduce_scatter | solution.py:174
  187.6 108.3 %reduce-scatter.8.cloned.1.call-start = ((), (), s32[]{:S(2)}) async-start(), calls=%async_computation.8 | async-start | bytes 1310720 | tf_op jit(solution)/shard_map/reduce_scatter | solution.py:190
  214.5 39.3 %copy-start.15 = (bf16[64,2048]{1,0:T(8,128)(2,1)}, bf16[64,2048]{1,0:T(8,128)(2,1)S(1)}, u32[]{:S(2)}) copy-start(bf16[64,2048]{1,0:T(8,128)(2,1)S(1)} %fusion.36) | copy-start | bytes 786436
  215.2 28.3 %collective-permute-start.8 = (bf16[64,16]{0,1:T(8,128)(2,1)S(1)}, bf16[64,16]{0,1:T(8,128)(2,1)S(1)}, u32[]{:S(2)}, u32[]{:S(2)}) collective-permute-start(bf16[64,16]{0,1:T(8,128)(2,1)S(1)} %bitcast.146), channel_id=1, source_target_pairs={{0,4},{4,8},{8,12},{12,16},{16,20},{20,24},{24,28},{28,32},{32,36}... | collective-permute-start | bytes 6152 | tf_op jit(solution)/shard_map/ppermute | solution.py:18
  216.8 27.0 %collective-permute-start.9 = (bf16[64,16]{0,1:T(8,128)(2,1)S(1)}, bf16[64,16]{0,1:T(8,128)(2,1)S(1)}, u32[]{:S(2)}, u32[]{:S(2)}) collective-permute-start(bf16[64,16]{0,1:T(8,128)(2,1)S(1)} %bitcast.145), channel_id=1, source_target_pairs={{4,0},{8,4},{12,8},{16,12},{20,16},{24,20},{28,24},{32,28},{36,32}... | collective-permute-start | bytes 6152 | tf_op jit(solution)/shard_map/ppermute | solution.py:18
  218.2 13.4 %collective-permute-start.10 = (bf16[64,1]{0,1:T(2,128)(2,1)S(1)}, bf16[64,1]{0,1:T(2,128)(2,1)S(1)}, u32[]{:S(2)}, u32[]{:S(2)}) collective-permute-start(bf16[64,1]{0,1:T(2,128)(2,1)S(1)} %bitcast.152), channel_id=1, source_target_pairs={{28,0},{32,4},{36,8},{40,12},{44,16},{48,20},{52,24},{56,28},{60,3... | collective-permute-start | bytes 392 | tf_op jit(solution)/shard_map/ppermute | solution.py:18
  219.6 18.2 %collective-permute-start.12 = (bf16[64,1]{0,1:T(2,128)(2,1)S(1)}, bf16[64,1]{0,1:T(2,128)(2,1)S(1)}, u32[]{:S(2)}, u32[]{:S(2)}) collective-permute-start(bf16[64,1]{0,1:T(2,128)(2,1)S(1)} %bitcast.151), channel_id=1, source_target_pairs={{36,0},{40,4},{44,8},{48,12},{52,16},{56,20},{60,24},{64,28},{68,3... | collective-permute-start | bytes 392 | tf_op jit(solution)/shard_map/ppermute | solution.py:18
  221.1 9.2 %collective-permute-start.15 = (bf16[64,1]{1,0:T(8,128)(2,1)S(1)}, bf16[64,1]{1,0:T(8,128)(2,1)S(1)}, u32[]{:S(2)}, u32[]{:S(2)}) collective-permute-start(bf16[64,1]{1,0:T(8,128)(2,1)S(1)} %copy.255), channel_id=1, source_target_pairs={{0,28},{4,32},{8,36},{12,40},{16,44},{20,48},{24,52},{28,56},{32,6... | collective-permute-start | bytes 392 | tf_op jit(solution)/shard_map/ppermute | solution.py:18
  230.3 15.1 %collective-permute-start.11 = (bf16[64,128]{1,0:T(8,128)(2,1)S(1)}, bf16[64,128]{1,0:T(8,128)(2,1)S(1)}, u32[]{:S(2)}, u32[]{:S(2)}) collective-permute-start(bf16[64,128]{1,0:T(8,128)(2,1)S(1)} %bitcast.139), channel_id=1, source_target_pairs={{32,0},{36,4},{40,8},{44,12},{48,16},{52,20},{56,24},{60,28},{64,3... | collective-permute-start | bytes 49160 | tf_op jit(solution)/shard_map/ppermute | solution.py:18
  231.6 11.6 %collective-permute-start.13 = (bf16[64,1]{0,1:T(2,128)(2,1)S(1)}, bf16[64,1]{0,1:T(2,128)(2,1)S(1)}, u32[]{:S(2)}, u32[]{:S(2)}) collective-permute-start(bf16[64,1]{0,1:T(2,128)(2,1)S(1)} %bitcast.153), channel_id=1, source_target_pairs={{0,36},{4,40},{8,44},{12,48},{16,52},{20,56},{24,60},{28,64},{32,6... | collective-permute-start | bytes 392 | tf_op jit(solution)/shard_map/ppermute | solution.py:18
  237.8 7.7 %collective-permute-start.14 = (bf16[64,128]{1,0:T(8,128)(2,1)S(1)}, bf16[64,128]{1,0:T(8,128)(2,1)S(1)}, u32[]{:S(2)}, u32[]{:S(2)}) collective-permute-start(bf16[64,128]{1,0:T(8,128)(2,1)S(1)} %bitcast.140), channel_id=1, source_target_pairs={{0,32},{4,36},{8,40},{12,44},{16,48},{20,52},{24,56},{28,60},{32,6... | collective-permute-start | bytes 49160 | tf_op jit(solution)/shard_map/ppermute | solution.py:18
  282.0 65.0 %all-to-all-start = ((bf16[1024,64,16]{0,2,1:T(8,128)(2,1)}), bf16[1024,64,16]{0,2,1:T(8,128)(2,1)}, u32[]{:S(2)}, u32[]{:S(2)}) async-start(bf16[1024,64,16]{0,2,1:T(8,128)(2,1)} %broadcast_select_fusion), calls=%async_computation.1 | async-start | bytes 4194304 | tf_op jit(solution)/shard_map/all_to_all | solution.py:168
  295.9 29.8 %all-gather.8.cloned.1.call-start = ((), (), s32[]{:S(2)}) async-start(), calls=%async_computation.9 | async-start | bytes 1310720 | tf_op jit(solution)/shard_map/all_gather | solution.py:200
  298.2 220.7 %all-reduce.4.cloned.1.call-start = ((), (), s32[]{:S(2)}) async-start(), calls=%async_computation.10 | async-start | bytes 2228224 | tf_op jit(solution)/shard_map/psum | solution.py:208
  351.1 173.1 %copy-start.1 = (bf16[9,64,256]{2,1,0:T(8,128)(2,1)S(1)}, bf16[9,64,256]{2,1,0:T(8,128)(2,1)}, u32[]{:S(2)}) copy-start(bf16[9,64,256]{2,1,0:T(8,128)(2,1)} %param.17) | copy-start | bytes 884740
  (22 other events, 156.8 us)
Sparse Core Ops, SparseCore 0:
  11.2 27.1 reduce-scatter.3
  40.8 27.2 all-gather.3
  152.4 28.5 all-gather.5
  187.7 25.3 reduce-scatter.5
  261.5 28.6 reduce-scatter.7
  298.9 26.6 all-gather.7
  330.4 188.4 all-reduce.3
where the time goes:
time: 538 us; the launch traced here: 531 us
  waiting for transfers between devices  301 us (56%)
  local copies, waits for them, and re-layouts  81.2 us (15%)
  starting transfers between devices  74.1 us (14%)
  matrix products  31.6 us (6%)
  other arithmetic  27.6 us (5%)
  between operations  15.3 us (3%)
    psum x1, waiting for transfers between devices, shards(): lax.psum((reduce_part, spatial_part, expand_part), 'slide')  163 us
    ppermute x16, starting transfers between devices, passed_along(): return lax.ppermute(block, axis, route)  47.9 us
    unnamed x95, local copies, waits for them, and re-layouts  32.8 us
    reduce_scatter x1, waiting for transfers between devices, shards(): lax.psum_scatter(jnp.dot(reduce_weight, features, preferred_element_type=...  27.9 us
    all_gather x1, waiting for transfers between devices, shards(): first_all = lax.all_gather(first_grid, 'grp', axis=0, tiled=True)  27.6 us
    reduce_scatter x1, waiting for transfers between devices, shards(): lax.psum_scatter(jnp.einsum('cm,cn->mn', expand_weight, back_three, prefe...  24.7 us
    all_to_all x1, waiting for transfers between devices, shards(): lax.all_to_all(outgoing_groups, 'slide', split_axis=1, concat_axis=1, til...  19 us
    all_gather x1, waiting for transfers between devices, shards(): back_one_all = lax.all_gather(back_one, 'grp', axis=0, tiled=True)  18.4 us
  transfers between devices with their start and end apart: 24, of which 10 were waited for; matrix products, arithmetic and copies ran while one was open for 13% of the time, Pallas kernels for 0%

commit v1 on v0

v1 whole, which is shorter than its diff:
```python
import functools
import math

import jax
import jax.numpy as jnp
from jax import lax
from jax.experimental import pallas as pl
from jax.experimental.pallas import tpu as pltpu
from jax.sharding import PartitionSpec as P

F32 = jnp.float32
BF16 = jnp.bfloat16
KAPPA = math.sqrt(2.0 / math.pi)
CUBIC = 0.044715
VMEM_BYTES = 48 * 1024 * 1024

GRID_R = 8
GRID_C = 8
N_SLIDE = 64
N_GRP = 4
TILE_COLS = 32
WIDE = 128
ROWS = 4
OWN = ROWS * WIDE
CELLS = N_GRP * OWN
CH = 256
MID = 256
PARAM_ROWS = 16
TAPS = tuple((a, b) for a in (-1, 0, 1) for b in (-1, 0, 1))
GRAD_SCALE = 1.0 / math.sqrt(N_SLIDE * CELLS)
SP_ROWS = 144
MAT_ROWS = 64


def call(body, outs, *args, flops=0, scratch=(), smem=()):
    spec = pl.BlockSpec(memory_space=pltpu.VMEM)
    scalar = pl.BlockSpec(memory_space=pltpu.SMEM)
    moved = sum(math.prod(s) * jnp.dtype(d).itemsize for s, d in outs)
    moved += sum(math.prod(a.shape) * a.dtype.itemsize for a in args)
    return pl.pallas_call(
        body,
        out_shape=[jax.ShapeDtypeStruct(s, d) for s, d in outs],
        in_specs=[scalar if i in smem else spec for i in range(len(args))],
        out_specs=[spec] * len(outs),
        scratch_shapes=list(scratch),
        compiler_params=pltpu.CompilerParams(vmem_limit_bytes=VMEM_BYTES),
        cost_estimate=pl.CostEstimate(flops=flops, bytes_accessed=moved, transcendentals=0),
    )(*args)


def dot(lhs, rhs, left=1, right=0):
    return lax.dot_general(lhs, rhs, (((left,), (right,)), ((), ())), preferred_element_type=F32)


def act_parts(v):
    sq = v * v
    t = jnp.tanh(KAPPA * (v + CUBIC * (v * sq)))
    half = 0.5 * (1.0 + t)
    slope = half + (0.5 * KAPPA) * v * (1.0 - t * t) * (1.0 + (3.0 * CUBIC) * sq)
    return v * half, slope


def tile_mask(tissue_row):
    spread = (
        lax.broadcasted_iota(jnp.int32, (TILE_COLS, WIDE), 1) // 4
        == lax.broadcasted_iota(jnp.int32, (TILE_COLS, WIDE), 0)
    ).astype(F32)
    row = tissue_row.astype(F32)
    if row.shape[0] == 1:
        row = jnp.broadcast_to(row, (8, TILE_COLS))
    return dot(row, spread)[:1]


def lanes(shape):
    return lax.broadcasted_iota(jnp.int32, shape, len(shape) - 1)


def reduce_kernel(me, feat, weight, params, *outs):
    g = me[0]
    own = lanes((8, MID)) // (MID // N_GRP) == g
    par = jnp.where(own, params[...], 0.0)[:4]
    hi = par.astype(BF16)
    rest = par - hi.astype(F32)
    mid = rest.astype(BF16)
    low = (rest - mid.astype(F32)).astype(BF16)
    tail = jnp.concatenate(
        [hi.astype(F32), mid.astype(F32), low.astype(F32), jnp.zeros((4, MID), F32)], 0
    ).astype(BF16)
    for k in range(N_GRP):
        start = pl.multiple_of(((g + k) % N_GRP) * OWN, OWN)
        block = dot(weight[...], feat[:, pl.ds(start, OWN)])
        outs[k][:MID] = block.astype(BF16)
        outs[k][MID:, :MID] = tail
        outs[k][MID:, MID:] = jnp.zeros((PARAM_ROWS, OWN - MID), BF16)


def first_kernel(me, p0, p1, p2, p3, tissue, act_out, slope_out, cols_out, left_out, right_out):
    g = me[0]
    tails = [p[MID:, :MID].astype(F32) for p in (p0, p1, p2, p3)]
    rows = (tails[0] + tails[1]) + (tails[2] + tails[3])
    par = (rows[0:4] + rows[4:8]) + rows[8:12]
    par = jnp.concatenate([par, jnp.zeros((124, MID), F32)], 0)
    cols = par.T
    cols_out[...] = cols
    mask = tile_mask(tissue[pl.ds(g, 1), :])
    for lo in range(0, MID, 32):
        part = slice(lo, lo + 32)
        scale = cols[part, 0:1]
        shift = cols[part, 1:2]
        lane = lanes((32, WIDE))
        left = jnp.zeros((32, WIDE), F32)
        right = jnp.zeros((32, WIDE), F32)
        for r in range(ROWS):
            seg = slice(r * WIDE, (r + 1) * WIDE)
            total = (p0[part, seg].astype(F32) + p1[part, seg].astype(F32)) + (
                p2[part, seg].astype(F32) + p3[part, seg].astype(F32)
            )
            value, slope = act_parts(scale * total + shift)
            value = mask * value
            act_out[part, seg] = value.astype(BF16)
            slope_out[part, seg] = (scale * mask) * slope
            left = jnp.where(lane == r, value[:, 0:1], left)
            right = jnp.where(lane == r, value[:, WIDE - 1 :], right)
        left_out[part] = left.astype(BF16)
        right_out[part] = right.astype(BF16)


def edge_kernel(grid, left, right, up_out, down_out):
    lane = lanes((MID, WIDE))
    lf = left[...].astype(F32)
    rt = right[...].astype(F32)
    for out, r in ((up_out, 0), (down_out, ROWS - 1)):
        out[:, :WIDE] = grid[:, r * WIDE : (r + 1) * WIDE]
        side = jnp.where(lane == 0, lf[:, r : r + 1], jnp.where(lane == 1, rt[:, r : r + 1], 0.0))
        out[:, WIDE:] = side.astype(BF16)


def shifted(grid, left, right, above, below, out):
    lane = lanes((MID, WIDE))
    lf = left[...].astype(F32)
    rt = right[...].astype(F32)
    ab = above[...].astype(F32)
    be = below[...].astype(F32)
    for r in range(ROWS + 2):
        seg = slice(r * WIDE, (r + 1) * WIDE)
        if r == 0:
            row, lcol, rcol = ab[:, :WIDE], ab[:, WIDE : WIDE + 1], ab[:, WIDE + 1 : WIDE + 2]
        elif r == ROWS + 1:
            row, lcol, rcol = be[:, :WIDE], be[:, WIDE : WIDE + 1], be[:, WIDE + 1 : WIDE + 2]
        else:
            row = grid[:, (r - 1) * WIDE : r * WIDE].astype(F32)
            lcol, rcol = lf[:, r - 1 : r], rt[:, r - 1 : r]
        out[1, :, seg] = row.astype(BF16)
        out[0, :, seg] = jnp.where(lane == 0, lcol, pltpu.roll(row, 1, 1)).astype(BF16)
        out[2, :, seg] = jnp.where(lane == WIDE - 1, rcol, pltpu.roll(row, WIDE - 1, 1)).astype(BF16)


def second_kernel(me, grid, left, right, above, below, weight, cols, tissue, act_out, slope_out, win_out, acc):
    shifted(grid, left, right, above, below, win_out)
    for t, (a, b) in enumerate(TAPS):
        w = jnp.concatenate([weight[q, t] for q in range(N_GRP)], 0)
        start = (a + 1) * WIDE
        part = dot(w, win_out[b + 1, :, start : start + OWN])
        acc[...] = part if t == 0 else acc[...] + part
    mask = tile_mask(tissue[pl.ds(me[0], 1), :])
    for lo in range(0, MID, 32):
        part = slice(lo, lo + 32)
        scale = cols[part, 2:3]
        shift = cols[part, 3:4]
        for r in range(ROWS):
            seg = slice(r * WIDE, (r + 1) * WIDE)
            value, slope = act_parts(scale * acc[part, seg] + shift)
            act_out[part, seg] = (mask * value).astype(BF16)
            slope_out[part, seg] = (scale * mask) * slope


def expand_kernel(me, s0, s1, s2, s3, weight, feat, ups, params, tissue, out, err_out, b0, b1, b2, b3, grad_out, acc, back):
    g = me[0]
    par = jnp.concatenate([params[...], jnp.zeros((120, CH), F32)], 0).T
    grad = None
    for k, (s, b_out) in enumerate(((s0, b0), (s1, b1), (s2, b2), (s3, b3))):
        q = (g + N_GRP - k) % N_GRP
        base = pl.multiple_of(q * OWN, OWN)
        acc[...] = dot(weight[...], s[...])
        mask = tile_mask(tissue[pl.ds(q, 1), :])
        for lo in range(0, CH, 32):
            part = slice(lo, lo + 32)
            scale = par[part, 4:5]
            shift = par[part, 5:6]
            for r in range(ROWS):
                seg = pl.ds(pl.multiple_of(base + r * WIDE, WIDE), WIDE)
                here = slice(r * WIDE, (r + 1) * WIDE)
                pre = feat[part, seg].astype(F32) + scale * acc[part, here] + shift
                value, slope = act_parts(pre)
                err = slope * (mask * ups[part, seg].astype(F32))
                out[part, seg] = (mask * value).astype(BF16)
                err_out[part, seg] = err.astype(BF16)
                back[part, here] = (scale * err).astype(BF16)
        b_out[...] = dot(weight[...], back[...], 0, 0).astype(BF16)
        term = dot(back[...], s[...], 1, 1)
        grad = term if grad is None else grad + term
    put_matrix(grad_out, grad)


def put_matrix(out, matrix):
    for p in range(8):
        h, q = divmod(p, 4)
        out[p] = matrix[q * MAT_ROWS : (q + 1) * MAT_ROWS, h * WIDE : (h + 1) * WIDE].astype(BF16)


def pack_kernel(owner, out, packed):
    col_own = jnp.broadcast_to(owner[...], (WIDE, WIDE))
    sub = lax.broadcasted_iota(jnp.int32, (WIDE, WIDE), 0)
    lane = lanes((WIDE, WIDE))
    row_own = jnp.sum(jnp.where(sub == lane, col_own, 0), 0, keepdims=True)
    rank = jnp.sum(jnp.where((col_own == row_own) & (lane < sub), 1, 0), 1, keepdims=True)
    slot = jnp.broadcast_to(owner[...] * 4 + rank, (WIDE, WIDE))
    pick = lane % 64
    cell = 4 * (pick // 2) + 2 * (pick % 2)
    even = (sub == cell + lane // 64).astype(BF16)
    odd = (sub == cell + 1 - lane // 64).astype(BF16)
    target = []
    for x in range(N_GRP):
        mine = jnp.where(sub == x * TILE_COLS + pick // 2, slot, 0)
        spot = jnp.sum(mine, 0, keepdims=True) * 4 + pick[:1] % 2
        target.append(spot)
    upper = lanes((1, WIDE)) // 64
    low = lanes((CH, WIDE)) < 64
    for j in range(2):
        goal = jnp.concatenate([t + 2 * ((upper + j) % 2) for t in target], 1)
        column = lax.broadcasted_iota(jnp.int32, (4 * CH, OWN), 0)
        select = (column == goal).astype(F32).astype(BF16)
        for i in range(2):
            pieces = []
            for x in range(N_GRP):
                at = x * OWN + i * WIDE
                first = dot(out[:, at : at + WIDE], even)
                second = dot(out[:, at + 2 * WIDE : at + 3 * WIDE], odd)
                if j == 0:
                    pieces.append(jnp.where(low, first, second).astype(BF16))
                else:
                    pieces.append(jnp.where(low, second, first).astype(BF16))
            moved = dot(select, jnp.concatenate(pieces, 1), 1, 1).astype(BF16)
            ij = 2 * i + j
            for h in range(2):
                packed[:, h * 512 + ij * WIDE : h * 512 + (ij + 1) * WIDE] = moved[:, h * WIDE : (h + 1) * WIDE]


def unpack_kernel(packed, out):
    row = lax.broadcasted_iota(jnp.int32, (512, 512), 0)
    col = lanes((512, 512))
    order = (col == (row % 4) * WIDE + row // 4).astype(F32).astype(BF16)
    for h in range(2):
        out[h * 512 : (h + 1) * 512] = dot(order, packed[:, h * 512 : (h + 1) * 512], 1, 1).astype(BF16)


def back_second_kernel(b0, b1, b2, b3, slope, grid_out, left_out, right_out):
    for lo in range(0, MID, 32):
        part = slice(lo, lo + 32)
        lane = lanes((32, WIDE))
        left = jnp.zeros((32, WIDE), F32)
        right = jnp.zeros((32, WIDE), F32)
        for r in range(ROWS):
            seg = slice(r * WIDE, (r + 1) * WIDE)
            total = (b0[part, seg].astype(F32) + b1[part, seg].astype(F32)) + (
                b2[part, seg].astype(F32) + b3[part, seg].astype(F32)
            )
            value = slope[part, seg] * total
            grid_out[part, seg] = value.astype(BF16)
            left = jnp.where(lane == r, value[:, 0:1], left)
            right = jnp.where(lane == r, value[:, WIDE - 1 :], right)
        left_out[part] = left.astype(BF16)
        right_out[part] = right.astype(BF16)


def back_first_kernel(grid, left, right, above, below, weight, slope, back_out, win, acc):
    shifted(grid, left, right, above, below, win)
    for t, (a, b) in enumerate(TAPS):
        w = jnp.concatenate([weight[q, t] for q in range(N_GRP)], 0)
        start = (1 - a) * WIDE
        part = dot(w, win[1 - b, :, start : start + OWN], 0, 0)
        acc[...] = part if t == 0 else acc[...] + part
    back_out[...] = (slope[...] * acc[...]).astype(BF16)


def spatial_kernel(grid, win, expand_part, out):
    for t, (a, b) in enumerate(TAPS):
        start = (a + 1) * WIDE
        term = dot(grid[...], win[b + 1, :, start : start + OWN], 1, 1).astype(BF16)
        for q in range(N_GRP):
            for lo in range(0, 64, 16):
                row = t * 64 + lo
                block, within = divmod(row, SP_ROWS)
                piece = term[q * 64 + lo : q * 64 + lo + 16]
                for h in range(2):
                    at = q * SP_ROWS + within
                    out[h * 4 + block, at : at + 16] = piece[:, h * WIDE : (h + 1) * WIDE]
    out[:, N_GRP * SP_ROWS :] = expand_part[...]


def last_kernel(me, o0, o1, o2, o3, weight, feat, err, out, grad_out):
    g = me[0]
    grad = None
    for k, o in enumerate((o0, o1, o2, o3)):
        base = pl.multiple_of(((g + N_GRP - k) % N_GRP) * OWN, OWN)
        seg = pl.ds(base, OWN)
        out[:, seg] = (err[:, seg].astype(F32) + dot(weight[...], o[...], 0, 0)).astype(BF16)
        term = dot(o[...], feat[:, seg], 1, 1)
        grad = term if grad is None else grad + term
    put_matrix(grad_out, grad)


def early_sum_kernel(me, parts, x0, x1, x2, x3, matrix):
    g = me[0]
    for k, out in enumerate((x0, x1, x2, x3)):
        start = pl.multiple_of(((g + k) % N_GRP) * SP_ROWS, 16)
        total = parts[0, pl.ds(start, SP_ROWS)].astype(F32)
        for p in range(1, 8):
            total = total + parts[p, pl.ds(start, SP_ROWS)].astype(F32)
        out[...] = total.astype(BF16)
    total = parts[0, N_GRP * SP_ROWS :].astype(F32)
    for p in range(1, 8):
        total = total + parts[p, N_GRP * SP_ROWS :].astype(F32)
    matrix[...] = total.astype(BF16)


def plane_sum_kernel(x0, x1, x2, x3, expand_part, parts, out):
    spatial = (x0[...].astype(F32) + x1[...].astype(F32)) + (x2[...].astype(F32) + x3[...].astype(F32))
    total = parts[0].astype(F32)
    for p in range(1, 8):
        total = total + parts[p].astype(F32)
    spatial = spatial.astype(BF16)
    total = total.astype(BF16)
    for p in range(8):
        out[p, :SP_ROWS] = spatial
        out[p, SP_ROWS : SP_ROWS + MAT_ROWS] = expand_part[...]
        out[p, SP_ROWS + MAT_ROWS :] = total


def all_sum_kernel(parts, out):
    total = parts[0].astype(F32)
    for p in range(1, 8):
        total = total + parts[p].astype(F32)
    total = total.astype(BF16)
    for p in range(8):
        out[p] = total


def finish_kernel(parts, reduce_out, spatial_out, expand_out):
    for p in range(8):
        h, q = divmod(p, 4)
        seg = slice(h * WIDE, (h + 1) * WIDE)
        spatial_out[q * SP_ROWS : (q + 1) * SP_ROWS, seg] = parts[p, :SP_ROWS].astype(F32) * GRAD_SCALE
        rows = slice(q * MAT_ROWS, (q + 1) * MAT_ROWS)
        expand_out[rows, seg] = parts[p, SP_ROWS : SP_ROWS + MAT_ROWS].astype(F32) * GRAD_SCALE
        reduce_out[rows, seg] = parts[p, SP_ROWS + MAT_ROWS :].astype(F32) * GRAD_SCALE


def along_grp(block, step):
    return lax.ppermute(block, "grp", [(i, (i + step) % N_GRP) for i in range(N_GRP)])


def column_moves():
    east = []
    for d in range(N_SLIDE):
        if d % GRID_C != GRID_C - 1:
            east.append((d, d + 1))
    return east, [(b, a) for a, b in east]


def row_moves():
    south = []
    for d in range(N_SLIDE):
        for g in range(N_GRP):
            if g < N_GRP - 1:
                south.append((d * N_GRP + g, d * N_GRP + g + 1))
            elif d // GRID_C < GRID_R - 1:
                south.append((d * N_GRP + g, (d + GRID_C) * N_GRP))
    return south, [(b, a) for a, b in south]


def halo(grid, left_strip, right_strip):
    east, west = column_moves()
    south, north = row_moves()
    left = lax.ppermute(right_strip, "slide", east)
    right = lax.ppermute(left_strip, "slide", west)
    up_msg, down_msg = call(edge_kernel, [((MID, 2 * WIDE), BF16)] * 2, grid, left, right)
    above = lax.ppermute(down_msg, ("slide", "grp"), south)
    below = lax.ppermute(up_msg, ("slide", "grp"), north)
    return left, right, above, below


PLANE = [[z * 8 + k for k in range(8)] for z in range(8)]
COLUMN = [[z * 8 + k for z in range(8)] for k in range(8)]


def exchange(pieces, groups):
    return lax.all_to_all(
        pieces, "slide", split_axis=0, concat_axis=0, axis_index_groups=groups, tiled=False
    )


def shards(
    features,
    tissue,
    group_owner,
    reduce_weight,
    spatial_weight,
    expand_weight,
    reduce_scale,
    reduce_shift,
    spatial_scale,
    spatial_shift,
    expand_scale,
    expand_shift,
    upstream,
):
    me = lax.axis_index("grp").astype(jnp.int32).reshape(1)
    own = (MID, OWN)
    weights = lax.all_gather(spatial_weight, "grp", axis=0, tiled=False)
    zero = jnp.zeros((CH,), F32)
    params = jnp.stack(
        [jnp.tile(v, N_GRP) for v in (reduce_scale, reduce_shift, spatial_scale, spatial_shift)]
        + [expand_scale, expand_shift, zero, zero]
    )
    with jax.named_scope("reduce"):
        p = call(
            reduce_kernel,
            [((MID + PARAM_ROWS, OWN), BF16)] * 4,
            me, features, reduce_weight, params,
            smem=(0,), flops=2 * MID * CH * CELLS,
        )
        p = [p[0]] + [along_grp(p[k], k) for k in (1, 2, 3)]
    with jax.named_scope("first"):
        first, slope_one, cols, left, right = call(
            first_kernel,
            [(own, BF16), (own, F32), ((MID, WIDE), F32), ((MID, WIDE), BF16), ((MID, WIDE), BF16)],
            me, *p, tissue,
            smem=(0,), flops=40 * MID * OWN,
        )
        edges = halo(first, left, right)
    with jax.named_scope("second"):
        second, slope_two, win = call(
            second_kernel,
            [(own, BF16), (own, F32), ((3, MID, OWN + 2 * WIDE), BF16)],
            me, first, *edges, weights, cols, tissue,
            smem=(0,), flops=18 * MID * MID * OWN, scratch=[pltpu.VMEM(own, F32)],
        )
        s = [second] + [along_grp(second, k) for k in (1, 2, 3)]
    with jax.named_scope("expand"):
        output, err, b0, b1, b2, b3, expand_part = call(
            expand_kernel,
            [((CH, CELLS), BF16), ((CH, CELLS), BF16)] + [(own, BF16)] * 4 + [((8, MAT_ROWS, WIDE), BF16)],
            me, *s, expand_weight, features, upstream, params, tissue,
            smem=(0,), flops=6 * CH * MID * CELLS,
            scratch=[pltpu.VMEM(own, F32), pltpu.VMEM(own, BF16)],
        )
        b = [b0] + [along_grp(v, -k) for k, v in ((1, b1), (2, b2), (3, b3))]
    with jax.named_scope("merge"):
        packed, = call(
            pack_kernel, [((4 * CH, 4 * CH), BF16)], group_owner, output,
            flops=8 * CH * 4 * CH * OWN,
        )
        arrived = lax.all_to_all(
            packed.reshape(N_SLIDE, 16, 4 * CH), "slide", split_axis=0, concat_axis=0, tiled=False
        ).reshape(4 * CH, 4 * CH)
        merged, = call(
            unpack_kernel, [((4 * CH, 4 * CH), BF16)], arrived, flops=4 * 512 * 512 * 4 * CH,
        )
    with jax.named_scope("back_second"):
        back_two, left, right = call(
            back_second_kernel,
            [(own, BF16), ((MID, WIDE), BF16), ((MID, WIDE), BF16)],
            *b, slope_two, flops=10 * MID * OWN,
        )
        edges = halo(back_two, left, right)
    with jax.named_scope("back_first"):
        back_one, = call(
            back_first_kernel,
            [(own, BF16)],
            back_two, *edges, weights, slope_one,
            flops=18 * MID * MID * OWN,
            scratch=[pltpu.VMEM((3, MID, OWN + 2 * WIDE), BF16), pltpu.VMEM(own, F32)],
        )
        o = [back_one] + [along_grp(back_one, k) for k in (1, 2, 3)]
    with jax.named_scope("spatial"):
        early, = call(
            spatial_kernel,
            [((8, N_GRP * SP_ROWS + MAT_ROWS, WIDE), BF16)],
            back_two, win, expand_part, flops=18 * MID * MID * OWN,
        )
        early = exchange(early, PLANE)
        x0, x1, x2, x3, expand_part = call(
            early_sum_kernel,
            [((SP_ROWS, WIDE), BF16)] * 4 + [((MAT_ROWS, WIDE), BF16)],
            me, early, smem=(0,),
        )
        x = [x0] + [along_grp(v, k) for k, v in ((1, x1), (2, x2), (3, x3))]
    with jax.named_scope("last"):
        feature_grad, reduce_part = call(
            last_kernel,
            [((CH, CELLS), BF16), ((8, MAT_ROWS, WIDE), BF16)],
            me, *o, reduce_weight, features, err,
            smem=(0,), flops=4 * CH * MID * CELLS,
        )
    with jax.named_scope("grads"):
        late = exchange(reduce_part, PLANE)
        height = SP_ROWS + 2 * MAT_ROWS
        plane, = call(plane_sum_kernel, [((8, height, WIDE), BF16)], *x, expand_part, late)
        total, = call(all_sum_kernel, [((8, height, WIDE), BF16)], exchange(plane, COLUMN))
        reduce_grad, spatial_grad, expand_grad = call(
            finish_kernel,
            [((MID, CH), F32), ((9 * 64, MID), F32), ((CH, MID), F32)],
            exchange(total, PLANE),
        )
    return merged, feature_grad, reduce_grad, spatial_grad.reshape(9, 64, MID), expand_grad


def solution(mesh):
    return jax.shard_map(
        shards,
        mesh=mesh,
        in_specs=(
            P("grp", "slide"),
            P("slide", None),
            P("slide", None),
            P(None, "grp"),
            P(None, "grp", None),
            P("grp", None),
            P("grp"),
            P("grp"),
            P("grp"),
            P("grp"),
            P("grp"),
            P("grp"),
            P("grp", "slide"),
        ),
        out_specs=(
            P("grp", "slide"),
            P("grp", "slide"),
            P(None, "grp"),
            P(None, "grp", None),
            P("grp", None),
        ),
        check_vma=False,
    )
```

time: 538 us -> 277 us (0.51)
  waiting for transfers between devices: 301 us -> 118 us
  local copies, waits for them, and re-layouts: 81.2 us -> 11.8 us
  matrix products: 31.6 us -> 0 us
  other arithmetic: 27.6 us -> 0 us
  blocking collectives: 0 us -> 25.3 us
  Pallas kernels: 0 us -> 18.6 us
  starting transfers between devices: 74.1 us -> 86.9 us
    psum x1 -> x0, waiting for transfers between devices: 163 us -> none  [shards(): lax.psum((reduce_part, spatial_part, expand_part), 'slide')]
    all_gather x3 -> x1, waiting for transfers between devices: 60.2 us -> 0.01 us  [shards(): weights = lax.all_gather(spatial_weight, 'grp', axis=0, tiled=False)]
    ppermute x16 -> x23, waiting for transfers between devices: 6.4 us -> 59.5 us  [the longest x15 43.7 us: along_grp(): lax.ppermute(block, 'grp', [(i, (i + step) % N_GRP) for i in range(N_GRP)])]
    reduce_scatter x3 -> x0, waiting for transfers between devices: 52.6 us -> none  [the longest x1 27.9 us: shards(): lax.psum_scatter(jnp.dot(reduce_weight, features, preferred_element_type=...]
    all_to_all x1 -> x4, waiting for transfers between devices: 19 us -> 57.6 us  [the longest x1 50.3 us: shards(): lax.all_to_all(packed.reshape(N_SLIDE, 16, 4 * CH), 'slide', split_axis=0...]
    dot_general x9 -> x0, matrix products: 31.6 us -> none  [the longest x1 7.55 us: shards(): jnp.einsum('on,tin->toi', back_two, columns, preferred_element_type=jnp.f...]
    all_to_all x0 -> x1, blocking collectives: none -> 25.3 us  [exchange(): lax.all_to_all(pieces, 'slide', split_axis=0, concat_axis=0, axis_index_g...]
    unnamed x95 -> x31, local copies, waits for them, and re-layouts: 32.8 us -> 8.17 us
  transfers between devices with their start and end apart: 24 -> 28, of which waited for: 10 -> 21; matrix products, arithmetic and copies ran while one was open for 13% -> 1% of each run, Pallas kernels for 0% -> 3%
where the time goes in v1:
time: 277 us; the launch traced here: 275 us
  waiting for transfers between devices  118 us (43%)
  starting transfers between devices  86.9 us (31%)
  blocking collectives  25.3 us (9%)
  Pallas kernels  18.6 us (7%)
  between operations  14.3 us (5%)
  local copies, waits for them, and re-layouts  11.8 us (4%)
    all_to_all x1, waiting for transfers between devices, shards(): lax.all_to_all(packed.reshape(N_SLIDE, 16, 4 * CH), 'slide', split_axis=0...  50.3 us
    ppermute x15, waiting for transfers between devices, along_grp(): lax.ppermute(block, 'grp', [(i, (i + step) % N_GRP) for i in range(N_GRP)])  43.7 us
    ppermute x15, starting transfers between devices, along_grp(): lax.ppermute(block, 'grp', [(i, (i + step) % N_GRP) for i in range(N_GRP)])  34.4 us
    all_to_all x3, starting transfers between devices, exchange(): lax.all_to_all(pieces, 'slide', split_axis=0, concat_axis=0, axis_index_g...  29.4 us
    all_to_all x1, blocking collectives, exchange(): lax.all_to_all(pieces, 'slide', split_axis=0, concat_axis=0, axis_index_g...  25.3 us
    pallas_call x16, Pallas kernels, call(): pl.pallas_call(body, out_shape=[jax.ShapeDtypeStruct(s, d) for s, d in ou...  18.6 us
    unnamed x31, local copies, waits for them, and re-layouts  8.17 us
    ppermute x2, starting transfers between devices, halo(): above = lax.ppermute(down_msg, ('slide', 'grp'), south)  7.35 us
  transfers between devices with their start and end apart: 28, of which 21 were waited for; matrix products, arithmetic and copies ran while one was open for 1% of the time, Pallas kernels for 3%

profile of v1, /device:TPU:2, one launch (start us, length us, event | category | flops | bytes accessed | tf_op | source)
XLA Modules:
  0.0 274.7 jit_solution(16112773942899027840)
XLA Ops:
  15.7 2.8 %collective-permute-start.1 = (bf16[272,512]{1,0:T(8,128)(2,1)S(1)}, bf16[272,512]{1,0:T(8,128)(2,1)S(1)}, u32[]{:S(2)}, u32[]{:S(2)}) collective-permute-start(bf16[272,512]{1,0:T(8,128)(2,1)S(1)} %get-tuple-element.43), channel_id=1, source_target_pairs={{0,2},{1,3},{2,0},{3,1},{4,6},{5,7},{6,4},{7,5},{8,10},{9,11},{10,... | collective-permute-start | bytes 835592 | tf_op jit(solution)/shard_map/reduce/ppermute | solution.py:360
  19.0 5.1 %collective-permute-done.p1 = bf16[272,512]{1,0:T(8,128)(2,1)S(1)} collective-permute-done((bf16[272,512]{1,0:T(8,128)(2,1)S(1)}, bf16[272,512]{1,0:T(8,128)(2,1)S(1)}, u32[]{:S(2)}, u32[]{:S(2)}) %collective-permute-start) | collective-permute-done | bytes 278560 | tf_op jit(solution)/shard_map/reduce/ppermute | solution.py:360
  24.1 2.8 %collective-permute-done.1.p2 = bf16[272,512]{1,0:T(8,128)(2,1)S(1)} collective-permute-done((bf16[272,512]{1,0:T(8,128)(2,1)S(1)}, bf16[272,512]{1,0:T(8,128)(2,1)S(1)}, u32[]{:S(2)}, u32[]{:S(2)}) %collective-permute-start.1) | collective-permute-done | bytes 278560 | tf_op jit(solution)/shard_map/reduce/ppermute | solution.py:360
  26.8 7.4 %collective-permute-done.2.p3 = bf16[272,512]{1,0:T(8,128)(2,1)S(1)} collective-permute-done((bf16[272,512]{1,0:T(8,128)(2,1)S(1)}, bf16[272,512]{1,0:T(8,128)(2,1)S(1)}, u32[]{:S(2)}, u32[]{:S(2)}) %collective-permute-start.2) | collective-permute-done | bytes 278560 | tf_op jit(solution)/shard_map/reduce/ppermute | solution.py:360
  37.9 3.8 %collective-permute-done.4.right = bf16[256,128]{1,0:T(8,128)(2,1)S(1)} collective-permute-done((bf16[256,128]{1,0:T(8,128)(2,1)S(1)}, bf16[256,128]{1,0:T(8,128)(2,1)S(1)}, u32[]{:S(2)}, u32[]{:S(2)}) %collective-permute-start.4) | collective-permute-done | bytes 65568 | tf_op jit(solution)/shard_map/first/ppermute | solution.py:386
  41.9 4.0 %collective-permute-start.5 = (bf16[256,256]{1,0:T(8,128)(2,1)S(1)}, bf16[256,256]{1,0:T(8,128)(2,1)S(1)}, u32[]{:S(2)}, u32[]{:S(2)}) collective-permute-start(bf16[256,256]{1,0:T(8,128)(2,1)S(1)} %get-tuple-element.48), channel_id=1, source_target_pairs={{0,1},{1,2},{2,3},{3,32},{4,5},{5,6},{6,7},{7,36},{8,9},{9,10},{10... | collective-permute-start | bytes 393224 | tf_op jit(solution)/shard_map/first/ppermute | solution.py:388
  48.9 3.9 %collective-permute-done.6.below = bf16[256,256]{1,0:T(8,128)(2,1)S(1)} collective-permute-done((bf16[256,256]{1,0:T(8,128)(2,1)S(1)}, bf16[256,256]{1,0:T(8,128)(2,1)S(1)}, u32[]{:S(2)}, u32[]{:S(2)}) %collective-permute-start.6) | collective-permute-done | bytes 131104 | tf_op jit(solution)/shard_map/first/ppermute | solution.py:389
  56.5 3.7 %collective-permute-start.8 = (bf16[256,512]{1,0:T(8,128)(2,1)S(1)}, bf16[256,512]{1,0:T(8,128)(2,1)S(1)}, u32[]{:S(2)}, u32[]{:S(2)}) collective-permute-start(bf16[256,512]{1,0:T(8,128)(2,1)S(1)} %get-tuple-element.51.s0), channel_id=1, source_target_pairs={{0,2},{1,3},{2,0},{3,1},{4,6},{5,7},{6,4},{7,5},{8,10},{9,11},{10,... | collective-permute-start | bytes 786440 | tf_op jit(solution)/shard_map/second/ppermute | solution.py:360
  60.2 2.5 collective-permute-start.9
  64.1 2.5 collective-permute-done.8.s2
  66.6 6.3 %collective-permute-done.9.s3 = bf16[256,512]{1,0:T(8,128)(2,1)S(1)} collective-permute-done((bf16[256,512]{1,0:T(8,128)(2,1)S(1)}, bf16[256,512]{1,0:T(8,128)(2,1)S(1)}, u32[]{:S(2)}, u32[]{:S(2)}) %collective-permute-start.9) | collective-permute-done | bytes 262176 | tf_op jit(solution)/shard_map/second/ppermute | solution.py:360
  72.9 4.6 %expand.1 = (bf16[256,2048]{1,0:T(8,128)(2,1)S(1)}, bf16[256,2048]{1,0:T(8,128)(2,1)S(1)}, bf16[256,512]{1,0:T(8,128)(2,1)S(1)}, bf16[256,512]{1,0:T(8,128)(2,1)...) custom-call(s32[1]{0:T(128)} %bitcast.me, ...), custom_call_target="tpu_custom_call" | custom-call | flops 805306368 | bytes 6562308 | tf_op jit(solution)/shard_map/expand/pallas_call | solution.py:40
  82.1 2.6 collective-permute-start.12
  84.7 2.6 collective-permute-done.10.b1
  87.3 7.0 %collective-permute-done.11.b2 = bf16[256,512]{1,0:T(8,128)(2,1)S(1)} collective-permute-done((bf16[256,512]{1,0:T(8,128)(2,1)S(1)}, bf16[256,512]{1,0:T(8,128)(2,1)S(1)}, u32[]{:S(2)}, u32[]{:S(2)}) %collective-permute-start.11) | collective-permute-done | bytes 262176 | tf_op jit(solution)/shard_map/expand/ppermute | solution.py:360
  97.4 6.0 %all-to-all-start.1 = ((bf16[8,640,128]{2,1,0:T(8,128)(2,1)}), bf16[8,640,128]{2,1,0:T(8,128)(2,1)S(1)}, u32[]{:S(2)}, u32[]{:S(2)}) async-start(bf16[8,640,128]{2,1,0:T(8,128)(2,1)} %copy-done.2), calls=%async_computation.1 | async-start | bytes 2621440 | tf_op jit(solution)/shard_map/spatial/all_to_all | solution.py:398
  107.1 3.0 %collective-permute-done.14.right = bf16[256,128]{1,0:T(8,128)(2,1)S(1)} collective-permute-done((bf16[256,128]{1,0:T(8,128)(2,1)S(1)}, bf16[256,128]{1,0:T(8,128)(2,1)S(1)}, u32[]{:S(2)}, u32[]{:S(2)}) %collective-permute-start.14) | collective-permute-done | bytes 65568 | tf_op jit(solution)/shard_map/back_second/ppermute | solution.py:386
  110.2 3.3 %collective-permute-start.15 = (bf16[256,256]{1,0:T(8,128)(2,1)S(1)}, bf16[256,256]{1,0:T(8,128)(2,1)S(1)}, u32[]{:S(2)}, u32[]{:S(2)}) collective-permute-start(bf16[256,256]{1,0:T(8,128)(2,1)S(1)} %get-tuple-element.61), channel_id=1, source_target_pairs={{0,1},{1,2},{2,3},{3,32},{4,5},{5,6},{6,7},{7,36},{8,9},{9,10},{10... | collective-permute-start | bytes 393224 | tf_op jit(solution)/shard_map/back_second/ppermute | solution.py:388
  113.6 2.8 %collective-permute-start.16 = (bf16[256,256]{1,0:T(8,128)(2,1)S(1)}, bf16[256,256]{1,0:T(8,128)(2,1)S(1)}, u32[]{:S(2)}, u32[]{:S(2)}) collective-permute-start(bf16[256,256]{1,0:T(8,128)(2,1)S(1)} %get-tuple-element.62), channel_id=1, source_target_pairs={{1,0},{2,1},{3,2},{32,3},{5,4},{6,5},{7,6},{36,7},{9,8},{10,9},{11... | collective-permute-start | bytes 393224 | tf_op jit(solution)/shard_map/back_second/ppermute | solution.py:389
  117.3 3.1 %collective-permute-done.16.below = bf16[256,256]{1,0:T(8,128)(2,1)S(1)} collective-permute-done((bf16[256,256]{1,0:T(8,128)(2,1)S(1)}, bf16[256,256]{1,0:T(8,128)(2,1)S(1)}, u32[]{:S(2)}, u32[]{:S(2)}) %collective-permute-start.16) | collective-permute-done | bytes 131104 | tf_op jit(solution)/shard_map/back_second/ppermute | solution.py:389
  123.0 3.9 %collective-permute-start.17 = (bf16[256,512]{1,0:T(8,128)(2,1)S(1)}, bf16[256,512]{1,0:T(8,128)(2,1)S(1)}, u32[]{:S(2)}, u32[]{:S(2)}) collective-permute-start(bf16[256,512]{1,0:T(8,128)(2,1)S(1)} %back_first.1.o0), channel_id=1, source_target_pairs={{0,1},{1,2},{2,3},{3,0},{4,5},{5,6},{6,7},{7,4},{8,9},{9,10},{10,1... | collective-permute-start | bytes 786440 | tf_op jit(solution)/shard_map/back_first/ppermute | solution.py:360
  126.9 3.7 %collective-permute-start.18 = (bf16[256,512]{1,0:T(8,128)(2,1)S(1)}, bf16[256,512]{1,0:T(8,128)(2,1)S(1)}, u32[]{:S(2)}, u32[]{:S(2)}) collective-permute-start(bf16[256,512]{1,0:T(8,128)(2,1)S(1)} %back_first.1.o0), channel_id=1, source_target_pairs={{0,2},{1,3},{2,0},{3,1},{4,6},{5,7},{6,4},{7,5},{8,10},{9,11},{10,... | collective-permute-start | bytes 786440 | tf_op jit(solution)/shard_map/back_first/ppermute | solution.py:360
  130.6 2.5 collective-permute-start.19
  133.1 3.3 %collective-permute-done.18.o2 = bf16[256,512]{1,0:T(8,128)(2,1)S(1)} collective-permute-done((bf16[256,512]{1,0:T(8,128)(2,1)S(1)}, bf16[256,512]{1,0:T(8,128)(2,1)S(1)}, u32[]{:S(2)}, u32[]{:S(2)}) %collective-permute-start.18) | collective-permute-done | bytes 262176 | tf_op jit(solution)/shard_map/back_first/ppermute | solution.py:360
  140.3 19.0 %all-to-all-start.2 = ((bf16[8,64,128]{2,1,0:T(8,128)(2,1)}), bf16[8,64,128]{2,1,0:T(8,128)(2,1)S(1)}, u32[]{:S(2)}, u32[]{:S(2)}) async-start(bf16[8,64,128]{2,1,0:T(8,128)(2,1)} %get-tuple-element.73), calls=%async_computation.2 | async-start | bytes 262144 | tf_op jit(solution)/shard_map/grads/all_to_all | solution.py:398
  160.1 3.7 %collective-permute-start.21 = (bf16[144,128]{1,0:T(8,128)(2,1)S(1)}, bf16[144,128]{1,0:T(8,128)(2,1)S(1)}, u32[]{:S(2)}, u32[]{:S(2)}) collective-permute-start(bf16[144,128]{1,0:T(8,128)(2,1)S(1)} %get-tuple-element.70), channel_id=1, source_target_pairs={{0,2},{1,3},{2,0},{3,1},{4,6},{5,7},{6,4},{7,5},{8,10},{9,11},{10,... | collective-permute-start | bytes 110600 | tf_op jit(solution)/shard_map/spatial/ppermute | solution.py:360
  167.8 25.3 %all_to_all.25.parts = bf16[8,272,128]{2,1,0:T(8,128)(2,1)S(1)} all-to-all(bf16[8,272,128]{2,1,0:T(8,128)(2,1)S(1)} %grads.3), channel_id=1, replica_groups={{0,32,64,96,128,160,192,224},{4,36,68,100,132,164,196,228},{8,40,72,104..., dimensions={0} | all-to-all | bytes 1114112 | tf_op jit(solution)/shard_map/grads/all_to_all | solution.py:398
  194.0 4.4 %all-to-all-start.4 = ((bf16[8,272,128]{2,1,0:T(8,128)(2,1)}), bf16[8,272,128]{2,1,0:T(8,128)(2,1)S(1)}, u32[]{:S(2)}, u32[]{:S(2)}) async-start(bf16[8,272,128]{2,1,0:T(8,128)(2,1)} %grads.4), calls=%async_computation.4 | async-start | bytes 1114112 | tf_op jit(solution)/shard_map/grads/all_to_all | solution.py:398
  201.9 7.2 %all-to-all-done.4.parts = bf16[8,272,128]{2,1,0:T(8,128)(2,1)S(1)} async-done(((bf16[8,272,128]{2,1,0:T(8,128)(2,1)}), bf16[8,272,128]{2,1,0:T(8,128)(2,1)S(1)}, u32[]{:S(2)}, u32[]{:S(2)}) %all-to-all-start.4) | async-done | bytes 557088 | tf_op jit(solution)/shard_map/grads/all_to_all | solution.py:398
  209.2 4.7 %all-to-all-start = ((bf16[64,16,1024]{2,1,0:T(8,128)(2,1)}), bf16[64,16,1024]{2,1,0:T(8,128)(2,1)S(1)}, u32[]{:S(2)}, u32[]{:S(2)}) async-start(bf16[64,16,1024]{2,1,0:T(8,128)(2,1)} %bitcast.8), calls=%async_computation | async-start | bytes 4194304 | tf_op jit(solution)/shard_map/merge/all_to_all | solution.py:464
  214.9 50.3 %all-to-all-done = bf16[64,16,1024]{2,1,0:T(8,128)(2,1)S(1)} async-done(((bf16[64,16,1024]{2,1,0:T(8,128)(2,1)}), bf16[64,16,1024]{2,1,0:T(8,128)(2,1)S(1)}, u32[]{:S(2)}, u32[]{:S(2)}) %all-to-all-start) | async-done | bytes 2097184 | tf_op jit(solution)/shard_map/merge/all_to_all | solution.py:464
  265.2 2.6 merge.3
  (83 shorter events, 50.0 us)
Async XLA Ops:
  7.2 27.1 %copy-start.11 = (s32[4,32]{1,0:T(4,128)S(1)}, s32[4,32]{1,0:T(4,128)}, u32[]{:S(2)}) copy-start(s32[4,32]{1,0:T(4,128)} %tissue.5) | copy-start | bytes 1540
  7.2 45.6 %all-gather.3.cloned.1.call-start = ((), (), s32[]{:S(2)}) async-start(), calls=%async_computation.5 | async-start | bytes 1474560 | tf_op jit(solution)/shard_map/all_gather | solution.py:420
  14.2 9.9 %collective-permute-start = (bf16[272,512]{1,0:T(8,128)(2,1)S(1)}, bf16[272,512]{1,0:T(8,128)(2,1)S(1)}, u32[]{:S(2)}, u32[]{:S(2)}) collective-permute-start(bf16[272,512]{1,0:T(8,128)(2,1)S(1)} %get-tuple-element.42), channel_id=1, source_target_pairs={{0,1},{1,2},{2,3},{3,0},{4,5},{5,6},{6,7},{7,4},{8,9},{9,10},{10,1... | collective-permute-start | bytes 835592 | tf_op jit(solution)/shard_map/reduce/ppermute | solution.py:360
  15.7 11.1 %collective-permute-start.1 = (bf16[272,512]{1,0:T(8,128)(2,1)S(1)}, bf16[272,512]{1,0:T(8,128)(2,1)S(1)}, u32[]{:S(2)}, u32[]{:S(2)}) collective-permute-start(bf16[272,512]{1,0:T(8,128)(2,1)S(1)} %get-tuple-element.43), channel_id=1, source_target_pairs={{0,2},{1,3},{2,0},{3,1},{4,6},{5,7},{6,4},{7,5},{8,10},{9,11},{10,... | collective-permute-start | bytes 835592 | tf_op jit(solution)/shard_map/reduce/ppermute | solution.py:360
  18.6 15.7 %collective-permute-start.2 = (bf16[272,512]{1,0:T(8,128)(2,1)S(1)}, bf16[272,512]{1,0:T(8,128)(2,1)S(1)}, u32[]{:S(2)}, u32[]{:S(2)}) collective-permute-start(bf16[272,512]{1,0:T(8,128)(2,1)S(1)} %get-tuple-element.44), channel_id=1, source_target_pairs={{0,3},{1,0},{2,1},{3,2},{4,7},{5,4},{6,5},{7,6},{8,11},{9,8},{10,9... | collective-permute-start | bytes 835592 | tf_op jit(solution)/shard_map/reduce/ppermute | solution.py:360
  34.3 38.7 %copy-start.10 = (bf16[256,256]{1,0:T(8,128)(2,1)S(1)}, bf16[256,256]{1,0:T(8,128)(2,1)}, u32[]{:S(2)}) copy-start(bf16[256,256]{1,0:T(8,128)(2,1)} %weight.4) | copy-start | bytes 393220
  35.3 2.6 collective-permute-start.3
  36.6 5.1 %collective-permute-start.4 = (bf16[256,128]{1,0:T(8,128)(2,1)S(1)}, bf16[256,128]{1,0:T(8,128)(2,1)S(1)}, u32[]{:S(2)}, u32[]{:S(2)}) collective-permute-start(bf16[256,128]{1,0:T(8,128)(2,1)S(1)} %get-tuple-element.47), channel_id=1, source_target_pairs={{4,0},{8,4},{12,8},{16,12},{20,16},{24,20},{28,24},{36,32},{40,36}... | collective-permute-start | bytes 196616 | tf_op jit(solution)/shard_map/first/ppermute | solution.py:386
  41.7 31.2 %copy-start.1 = (bf16[256,2048]{1,0:T(8,128)(2,1)S(1)}, bf16[256,2048]{1,0:T(8,128)(2,1)}, u32[]{:S(2)}) copy-start(bf16[256,2048]{1,0:T(8,128)(2,1)} %feat.5) | copy-start | bytes 3145732
  41.9 7.0 %collective-permute-start.5 = (bf16[256,256]{1,0:T(8,128)(2,1)S(1)}, bf16[256,256]{1,0:T(8,128)(2,1)S(1)}, u32[]{:S(2)}, u32[]{:S(2)}) collective-permute-start(bf16[256,256]{1,0:T(8,128)(2,1)S(1)} %get-tuple-element.48), channel_id=1, source_target_pairs={{0,1},{1,2},{2,3},{3,32},{4,5},{5,6},{6,7},{7,36},{8,9},{9,10},{10... | collective-permute-start | bytes 393224 | tf_op jit(solution)/shard_map/first/ppermute | solution.py:388
  45.9 6.9 %collective-permute-start.6 = (bf16[256,256]{1,0:T(8,128)(2,1)S(1)}, bf16[256,256]{1,0:T(8,128)(2,1)S(1)}, u32[]{:S(2)}, u32[]{:S(2)}) collective-permute-start(bf16[256,256]{1,0:T(8,128)(2,1)S(1)} %get-tuple-element.49), channel_id=1, source_target_pairs={{1,0},{2,1},{3,2},{32,3},{5,4},{6,5},{7,6},{36,7},{9,8},{10,9},{11... | collective-permute-start | bytes 393224 | tf_op jit(solution)/shard_map/first/ppermute | solution.py:389
  55.3 8.8 %collective-permute-start.7 = (bf16[256,512]{1,0:T(8,128)(2,1)S(1)}, bf16[256,512]{1,0:T(8,128)(2,1)S(1)}, u32[]{:S(2)}, u32[]{:S(2)}) collective-permute-start(bf16[256,512]{1,0:T(8,128)(2,1)S(1)} %get-tuple-element.51.s0), channel_id=1, source_target_pairs={{0,1},{1,2},{2,3},{3,0},{4,5},{5,6},{6,7},{7,4},{8,9},{9,10},{10,1... | collective-permute-start | bytes 786440 | tf_op jit(solution)/shard_map/second/ppermute | solution.py:360
  56.5 10.1 %collective-permute-start.8 = (bf16[256,512]{1,0:T(8,128)(2,1)S(1)}, bf16[256,512]{1,0:T(8,128)(2,1)S(1)}, u32[]{:S(2)}, u32[]{:S(2)}) collective-permute-start(bf16[256,512]{1,0:T(8,128)(2,1)S(1)} %get-tuple-element.51.s0), channel_id=1, source_target_pairs={{0,2},{1,3},{2,0},{3,1},{4,6},{5,7},{6,4},{7,5},{8,10},{9,11},{10,... | collective-permute-start | bytes 786440 | tf_op jit(solution)/shard_map/second/ppermute | solution.py:360
  60.2 12.8 %collective-permute-start.9 = (bf16[256,512]{1,0:T(8,128)(2,1)S(1)}, bf16[256,512]{1,0:T(8,128)(2,1)S(1)}, u32[]{:S(2)}, u32[]{:S(2)}) collective-permute-start(bf16[256,512]{1,0:T(8,128)(2,1)S(1)} %get-tuple-element.51.s0), channel_id=1, source_target_pairs={{0,3},{1,0},{2,1},{3,2},{4,7},{5,4},{6,5},{7,6},{8,11},{9,8},{10,9... | collective-permute-start | bytes 786440 | tf_op jit(solution)/shard_map/second/ppermute | solution.py:360
  78.6 17.0 %copy-start.6 = (bf16[256,2048]{1,0:T(8,128)(2,1)}, bf16[256,2048]{1,0:T(8,128)(2,1)S(1)}, u32[]{:S(2)}) copy-start(bf16[256,2048]{1,0:T(8,128)(2,1)S(1)} %get-tuple-element.64.err) | copy-start | bytes 3145732
  78.6 8.7 %collective-permute-start.10 = (bf16[256,512]{1,0:T(8,128)(2,1)S(1)}, bf16[256,512]{1,0:T(8,128)(2,1)S(1)}, u32[]{:S(2)}, u32[]{:S(2)}) collective-permute-start(bf16[256,512]{1,0:T(8,128)(2,1)S(1)} %get-tuple-element.54), channel_id=1, source_target_pairs={{0,3},{1,0},{2,1},{3,2},{4,7},{5,4},{6,5},{7,6},{8,11},{9,8},{10,9... | collective-permute-start | bytes 786440 | tf_op jit(solution)/shard_map/expand/ppermute | solution.py:360
  80.6 13.6 %collective-permute-start.11 = (bf16[256,512]{1,0:T(8,128)(2,1)S(1)}, bf16[256,512]{1,0:T(8,128)(2,1)S(1)}, u32[]{:S(2)}, u32[]{:S(2)}) collective-permute-start(bf16[256,512]{1,0:T(8,128)(2,1)S(1)} %get-tuple-element.55), channel_id=1, source_target_pairs={{0,2},{1,3},{2,0},{3,1},{4,6},{5,7},{6,4},{7,5},{8,10},{9,11},{10,... | collective-permute-start | bytes 786440 | tf_op jit(solution)/shard_map/expand/ppermute | solution.py:360
  82.1 13.1 %collective-permute-start.12 = (bf16[256,512]{1,0:T(8,128)(2,1)S(1)}, bf16[256,512]{1,0:T(8,128)(2,1)S(1)}, u32[]{:S(2)}, u32[]{:S(2)}) collective-permute-start(bf16[256,512]{1,0:T(8,128)(2,1)S(1)} %get-tuple-element.56), channel_id=1, source_target_pairs={{0,1},{1,2},{2,3},{3,0},{4,5},{5,6},{6,7},{7,4},{8,9},{9,10},{10,1... | collective-permute-start | bytes 786440 | tf_op jit(solution)/shard_map/expand/ppermute | solution.py:360
  97.4 42.9 %all-to-all-start.1 = ((bf16[8,640,128]{2,1,0:T(8,128)(2,1)}), bf16[8,640,128]{2,1,0:T(8,128)(2,1)S(1)}, u32[]{:S(2)}, u32[]{:S(2)}) async-start(bf16[8,640,128]{2,1,0:T(8,128)(2,1)} %copy-done.2), calls=%async_computation.1 | async-start | bytes 2621440 | tf_op jit(solution)/shard_map/spatial/all_to_all | solution.py:398
  103.4 3.7 %collective-permute-start.13 = (bf16[256,128]{1,0:T(8,128)(2,1)S(1)}, bf16[256,128]{1,0:T(8,128)(2,1)S(1)}, u32[]{:S(2)}, u32[]{:S(2)}) collective-permute-start(bf16[256,128]{1,0:T(8,128)(2,1)S(1)} %get-tuple-element.59), channel_id=1, source_target_pairs={{0,4},{4,8},{8,12},{12,16},{16,20},{20,24},{24,28},{32,36},{36,40}... | collective-permute-start | bytes 196616 | tf_op jit(solution)/shard_map/back_second/ppermute | solution.py:385
  105.8 4.3 %collective-permute-start.14 = (bf16[256,128]{1,0:T(8,128)(2,1)S(1)}, bf16[256,128]{1,0:T(8,128)(2,1)S(1)}, u32[]{:S(2)}, u32[]{:S(2)}) collective-permute-start(bf16[256,128]{1,0:T(8,128)(2,1)S(1)} %get-tuple-element.60), channel_id=1, source_target_pairs={{4,0},{8,4},{12,8},{16,12},{20,16},{24,20},{28,24},{36,32},{40,36}... | collective-permute-start | bytes 196616 | tf_op jit(solution)/shard_map/back_second/ppermute | solution.py:386
  110.2 7.1 %collective-permute-start.15 = (bf16[256,256]{1,0:T(8,128)(2,1)S(1)}, bf16[256,256]{1,0:T(8,128)(2,1)S(1)}, u32[]{:S(2)}, u32[]{:S(2)}) collective-permute-start(bf16[256,256]{1,0:T(8,128)(2,1)S(1)} %get-tuple-element.61), channel_id=1, source_target_pairs={{0,1},{1,2},{2,3},{3,32},{4,5},{5,6},{6,7},{7,36},{8,9},{9,10},{10... | collective-permute-start | bytes 393224 | tf_op jit(solution)/shard_map/back_second/ppermute | solution.py:388
  113.6 6.9 %collective-permute-start.16 = (bf16[256,256]{1,0:T(8,128)(2,1)S(1)}, bf16[256,256]{1,0:T(8,128)(2,1)S(1)}, u32[]{:S(2)}, u32[]{:S(2)}) collective-permute-start(bf16[256,256]{1,0:T(8,128)(2,1)S(1)} %get-tuple-element.62), channel_id=1, source_target_pairs={{1,0},{2,1},{3,2},{32,3},{5,4},{6,5},{7,6},{36,7},{9,8},{10,9},{11... | collective-permute-start | bytes 393224 | tf_op jit(solution)/shard_map/back_second/ppermute | solution.py:389
  123.0 10.1 %collective-permute-start.17 = (bf16[256,512]{1,0:T(8,128)(2,1)S(1)}, bf16[256,512]{1,0:T(8,128)(2,1)S(1)}, u32[]{:S(2)}, u32[]{:S(2)}) collective-permute-start(bf16[256,512]{1,0:T(8,128)(2,1)S(1)} %back_first.1.o0), channel_id=1, source_target_pairs={{0,1},{1,2},{2,3},{3,0},{4,5},{5,6},{6,7},{7,4},{8,9},{9,10},{10,1... | collective-permute-start | bytes 786440 | tf_op jit(solution)/shard_map/back_first/ppermute | solution.py:360
  126.9 9.5 %collective-permute-start.18 = (bf16[256,512]{1,0:T(8,128)(2,1)S(1)}, bf16[256,512]{1,0:T(8,128)(2,1)S(1)}, u32[]{:S(2)}, u32[]{:S(2)}) collective-permute-start(bf16[256,512]{1,0:T(8,128)(2,1)S(1)} %back_first.1.o0), channel_id=1, source_target_pairs={{0,2},{1,3},{2,0},{3,1},{4,6},{5,7},{6,4},{7,5},{8,10},{9,11},{10,... | collective-permute-start | bytes 786440 | tf_op jit(solution)/shard_map/back_first/ppermute | solution.py:360
  130.6 7.9 %collective-permute-start.19 = (bf16[256,512]{1,0:T(8,128)(2,1)S(1)}, bf16[256,512]{1,0:T(8,128)(2,1)S(1)}, u32[]{:S(2)}, u32[]{:S(2)}) collective-permute-start(bf16[256,512]{1,0:T(8,128)(2,1)S(1)} %back_first.1.o0), channel_id=1, source_target_pairs={{0,3},{1,0},{2,1},{3,2},{4,7},{5,4},{6,5},{7,6},{8,11},{9,8},{10,9... | collective-permute-start | bytes 786440 | tf_op jit(solution)/shard_map/back_first/ppermute | solution.py:360
  140.3 25.1 %all-to-all-start.2 = ((bf16[8,64,128]{2,1,0:T(8,128)(2,1)}), bf16[8,64,128]{2,1,0:T(8,128)(2,1)S(1)}, u32[]{:S(2)}, u32[]{:S(2)}) async-start(bf16[8,64,128]{2,1,0:T(8,128)(2,1)} %get-tuple-element.73), calls=%async_computation.2 | async-start | bytes 262144 | tf_op jit(solution)/shard_map/grads/all_to_all | solution.py:398
  159.4 6.0 %collective-permute-start.20 = (bf16[144,128]{1,0:T(8,128)(2,1)S(1)}, bf16[144,128]{1,0:T(8,128)(2,1)S(1)}, u32[]{:S(2)}, u32[]{:S(2)}) collective-permute-start(bf16[144,128]{1,0:T(8,128)(2,1)S(1)} %get-tuple-element.69), channel_id=1, source_target_pairs={{0,1},{1,2},{2,3},{3,0},{4,5},{5,6},{6,7},{7,4},{8,9},{9,10},{10,1... | collective-permute-start | bytes 110600 | tf_op jit(solution)/shard_map/spatial/ppermute | solution.py:360
  160.1 5.8 %collective-permute-start.21 = (bf16[144,128]{1,0:T(8,128)(2,1)S(1)}, bf16[144,128]{1,0:T(8,128)(2,1)S(1)}, u32[]{:S(2)}, u32[]{:S(2)}) collective-permute-start(bf16[144,128]{1,0:T(8,128)(2,1)S(1)} %get-tuple-element.70), channel_id=1, source_target_pairs={{0,2},{1,3},{2,0},{3,1},{4,6},{5,7},{6,4},{7,5},{8,10},{9,11},{10,... | collective-permute-start | bytes 110600 | tf_op jit(solution)/shard_map/spatial/ppermute | solution.py:360
  163.8 4.0 %collective-permute-start.22 = (bf16[144,128]{1,0:T(8,128)(2,1)S(1)}, bf16[144,128]{1,0:T(8,128)(2,1)S(1)}, u32[]{:S(2)}, u32[]{:S(2)}) collective-permute-start(bf16[144,128]{1,0:T(8,128)(2,1)S(1)} %get-tuple-element.71), channel_id=1, source_target_pairs={{0,3},{1,0},{2,1},{3,2},{4,7},{5,4},{6,5},{7,6},{8,11},{9,8},{10,9... | collective-permute-start | bytes 110600 | tf_op jit(solution)/shard_map/spatial/ppermute | solution.py:360
  194.0 15.1 %all-to-all-start.4 = ((bf16[8,272,128]{2,1,0:T(8,128)(2,1)}), bf16[8,272,128]{2,1,0:T(8,128)(2,1)S(1)}, u32[]{:S(2)}, u32[]{:S(2)}) async-start(bf16[8,272,128]{2,1,0:T(8,128)(2,1)} %grads.4), calls=%async_computation.4 | async-start | bytes 1114112 | tf_op jit(solution)/shard_map/grads/all_to_all | solution.py:398
  209.2 56.1 %all-to-all-start = ((bf16[64,16,1024]{2,1,0:T(8,128)(2,1)}), bf16[64,16,1024]{2,1,0:T(8,128)(2,1)S(1)}, u32[]{:S(2)}, u32[]{:S(2)}) async-start(bf16[64,16,1024]{2,1,0:T(8,128)(2,1)} %bitcast.8), calls=%async_computation | async-start | bytes 4194304 | tf_op jit(solution)/shard_map/merge/all_to_all | solution.py:464
  (11 other events, 52.4 us)
Sparse Core Ops, SparseCore 0:
  9.8 31.2 all-gather.2
